TPU v7x, 32 devices: a whole 2x2x4 slice. The times are simulated.
32 devices in a mesh: dp: 4 (over y, x), expert: 8 (over z, core).
Axes of the slice: x: 2, y: 2, z: 4, core: 2. Of those that a mesh axis runs over, the one named last changes fastest.
Arguments:
- tokens: bfloat16 [4096, 2048], P(('dp', 'expert')), may hold values from -6 to 6
- out_grad: bfloat16 [4096, 2048], P(('dp', 'expert')), may hold values from -6 to 6
- expert_ids: int32 [4096, 8], P(('dp', 'expert')), may hold values from 0 to 15, all different within a row
- route_probs: bfloat16 [4096, 8], P(('dp', 'expert')), may hold values from 0.019897461 to 0.5
- w_gate: bfloat16 [16, 2048, 768], P('expert'), may hold values from -0.125 to 0.125
- w_up: bfloat16 [16, 2048, 768], P('expert'), may hold values from -0.125 to 0.125
- w_down: bfloat16 [16, 2048, 768], P('expert'), may hold values from -0.21875 to 0.21875
- decay_mask: int32 [16, 3], P('expert'), may hold values from 0 to 1
Outputs:
- grad_tokens: bfloat16 [4096, 2048], P(('dp', 'expert'))
- grad_probs: bfloat16 [4096, 8], P(('dp', 'expert'))
- new_gate: bfloat16 [16, 2048, 768], P('expert', 'dp')
- new_up: bfloat16 [16, 2048, 768], P('expert', 'dp')
- new_down: bfloat16 [16, 2048, 768], P('expert', 'dp')
All inputs are finite; a program needn't handle non-finite values.
Results may differ from a plain program's by a relative error of at most 0.015.
Values may be sent and summed in bfloat16 or wider, within the bound.
A program may use at most 192 MiB of HBM per device.

v0:
```python
import jax
import jax.numpy as jnp
from jax import lax
from jax.sharding import PartitionSpec as P

step_size = 0.004
shrink_rate = 0.1


def body(tokens, out_grad, expert_ids, route_probs, w_gate, w_up, w_down, decay_mask):
    n_owner = lax.axis_size("expert")
    n_group = lax.axis_size("dp")
    local_exp = w_gate.shape[0]
    width = tokens.shape[1]
    hidden = w_gate.shape[2]
    tok_rows = tokens.shape[0]
    topk = expert_ids.shape[1]
    n_experts = n_owner * local_exp
    capacity = tok_rows * topk // n_experts
    assigns = tok_rows * topk
    flat_ids = expert_ids.reshape(assigns)
    onehot = (flat_ids[:, None] == jnp.arange(n_experts, dtype=jnp.int32)[None, :]).astype(
        jnp.int32
    )
    before = jnp.cumsum(onehot, axis=0) - onehot
    position = jnp.sum(before * onehot, axis=1)
    slots = jnp.where(position < capacity, flat_ids * capacity + position, n_experts * capacity)
    order = jnp.arange(assigns, dtype=jnp.int32)
    slot_token = (
        jnp.full((n_experts * capacity + 1,), tok_rows, jnp.int32).at[slots].set(order // topk)[:-1]
    )
    slot_assign = (
        jnp.full((n_experts * capacity + 1,), assigns, jnp.int32).at[slots].set(order)[:-1]
    )
    zero_row = jnp.zeros((1, width), jnp.bfloat16)
    tok_pad = jnp.concatenate([tokens, zero_row], axis=0)
    grad_pad = jnp.concatenate([out_grad, zero_row], axis=0)
    prob_pad = jnp.concatenate(
        [route_probs.reshape(assigns), jnp.zeros((1,), jnp.bfloat16)], axis=0
    )
    send_x = tok_pad[slot_token].reshape(n_owner, local_exp * capacity, width)
    send_dy = grad_pad[slot_token].reshape(n_owner, local_exp * capacity, width)
    send_p = prob_pad[slot_assign].reshape(n_owner, local_exp * capacity)
    got_x, got_dy, got_p = (
        lax.all_to_all(send_x, "expert", split_axis=0, concat_axis=0, tiled=True),
        lax.all_to_all(send_dy, "expert", split_axis=0, concat_axis=0, tiled=True),
        lax.all_to_all(send_p, "expert", split_axis=0, concat_axis=0, tiled=True),
    )
    rows_x = got_x.reshape(n_owner, local_exp, capacity, width)
    rows_dy = got_dy.reshape(n_owner, local_exp, capacity, width)
    rows_p = got_p.reshape(n_owner, local_exp, capacity)
    gate = jnp.einsum("sjcd,jdh->sjch", rows_x, w_gate, preferred_element_type=jnp.float32)
    upper = jnp.einsum("sjcd,jdh->sjch", rows_x, w_up, preferred_element_type=jnp.float32)
    sig = jax.nn.sigmoid(gate)
    act = gate * sig
    hid = (act * upper).astype(jnp.bfloat16)
    outs = jnp.einsum("sjch,jdh->sjcd", hid, w_down, preferred_element_type=jnp.float32).astype(
        jnp.bfloat16
    )
    dout = (rows_p[..., None].astype(jnp.float32) * rows_dy.astype(jnp.float32)).astype(
        jnp.bfloat16
    )
    dhid = jnp.einsum("sjcd,jdh->sjch", dout, w_down, preferred_element_type=jnp.float32)
    dgate = (dhid * upper * sig * (1.0 + gate * (1.0 - sig))).astype(jnp.bfloat16)
    dup = (dhid * act).astype(jnp.bfloat16)
    dx_slots = (
        jnp.einsum("sjch,jdh->sjcd", dgate, w_gate, preferred_element_type=jnp.float32)
        + jnp.einsum("sjch,jdh->sjcd", dup, w_up, preferred_element_type=jnp.float32)
    ).astype(jnp.bfloat16)
    dx_send = dx_slots.reshape(n_owner, local_exp * capacity, width)
    back_out = lax.all_to_all(
        outs.reshape(n_owner, local_exp * capacity, width),
        "expert",
        split_axis=0,
        concat_axis=0,
        tiled=True,
    )
    out_pad = jnp.concatenate([back_out.reshape(n_experts * capacity, width), zero_row], axis=0)
    routed_out = out_pad[slots].reshape(tok_rows, topk, width)
    grad_probs = jnp.einsum(
        "tkd,td->tk", routed_out, out_grad, preferred_element_type=jnp.float32
    ).astype(jnp.bfloat16)
    back_dx = lax.all_to_all(dx_send, "expert", split_axis=0, concat_axis=0, tiled=True)
    dx_pad = jnp.concatenate([back_dx.reshape(n_experts * capacity, width), zero_row], axis=0)
    routed_dx = dx_pad[slots].reshape(tok_rows, topk, width)
    grad_tokens = jnp.sum(routed_dx.astype(jnp.float32), axis=1).astype(jnp.bfloat16)
    shard_rows = width // n_group
    grad_g = jnp.einsum("sjcd,sjch->djh", rows_x, dgate, preferred_element_type=jnp.float32)
    grad_u = jnp.einsum("sjcd,sjch->djh", rows_x, dup, preferred_element_type=jnp.float32)
    grad_d = jnp.einsum("sjcd,sjch->djh", dout, hid, preferred_element_type=jnp.float32)
    stacked = jnp.stack([grad_g, grad_u, grad_d], axis=1)
    summed = lax.psum_scatter(
        stacked.reshape(shard_rows * lax.axis_size("dp"), 3 * local_exp * hidden).astype(
            jnp.bfloat16
        ),
        "dp",
        scatter_dimension=0,
        tiled=True,
    ).astype(jnp.float32)
    grads = summed.reshape(shard_rows, 3, local_exp, hidden).transpose(1, 2, 0, 3)
    first_row = lax.axis_index("dp") * shard_rows
    rates = decay_mask.astype(jnp.float32)

    def update(weight, grad_w, column):
        weight_f = lax.dynamic_slice_in_dim(weight, first_row, shard_rows, 1).astype(jnp.float32)
        factor = rates[:, column][:, None, None]
        return (weight_f - step_size * grad_w - shrink_rate * factor * weight_f).astype(
            jnp.bfloat16
        )

    new_gate = update(w_gate, grads[0], 0)
    new_up = update(w_up, grads[1], 1)
    new_down = update(w_down, grads[2], 2)
    return (grad_tokens, grad_probs, new_gate, new_up, new_down)


def solution(mesh):
    placed = (
        P(("dp", "expert"), None),
        P(("dp", "expert"), None),
        P(("dp", "expert"), None),
        P(("dp", "expert"), None),
        P("expert", None, None),
        P("expert", None, None),
        P("expert", None, None),
        P("expert", None),
    )
    return jax.shard_map(
        body,
        mesh=mesh,
        in_specs=placed,
        out_specs=(
            P(("dp", "expert"), None),
            P(("dp", "expert"), None),
            P("expert", "dp", None),
            P("expert", "dp", None),
            P("expert", "dp", None),
        ),
        check_vma=False,
    )
```

profile of v0, /device:TPU:0, one launch (start us, length us, event | category | flops | bytes accessed | tf_op | source)
XLA Modules:
  0.0 574.7 jit_solution(16490669030956403925)
XLA Ops:
  8.8 4.5 reduce-window.6
  14.9 4.3 scatter_custom_fusion
  19.3 6.8 %gather_fusion = bf16[1024]{0:T(1024)(128)(2,1)S(1)} fusion(bf16[1025]{0:T(1024)(128)(2,1)S(1)} %pad_maximum_fusion.1, s32[1024]{0:T(1024)S(1)} %fusion.54), kind=kCustom, calls=%fused_computation | custom fusion | bytes 8192 | tf_op jit(solution)/shard_map/gather | solution.py:43
  26.7 6.3 %all-to-all-start = ((bf16[8,1,128]{2,1,0:T(2,128)(2,1)}), bf16[8,1,128]{2,1,0:T(2,128)(2,1)S(1)}, u32[]{:S(2)}, u32[]{:S(2)}) async-start(bf16[8,1,128]{2,1,0:T(2,128)(2,1)} %copy.41), calls=%async_computation | async-start | bytes 8192 | tf_op jit(solution)/shard_map/all_to_all | solution.py:47
  33.0 4.3 scatter_custom_fusion.1
  38.5 6.1 %gather_fusion.2 = bf16[1024,2048]{1,0:T(8,128)(2,1)} fusion(bf16[129,2048]{1,0:T(8,128)(2,1)S(1)} %concatenate.17, s32[1024]{0:T(1024)S(1)} %fusion.55), kind=kCustom, calls=%fused_computation.2 | custom fusion | bytes 8392704 | tf_op jit(solution)/shard_map/gather | solution.py:41
  44.5 5.2 all-to-all-start.2
  49.8 6.0 %gather_fusion.1 = bf16[1024,2048]{1,0:T(8,128)(2,1)} fusion(bf16[129,2048]{1,0:T(8,128)(2,1)S(1)} %concatenate.16, s32[1024]{0:T(1024)S(1)} %fusion.55), kind=kCustom, calls=%fused_computation.1 | custom fusion | bytes 8392704 | tf_op jit(solution)/shard_map/gather | solution.py:42
  55.8 88.0 %all-to-all-done.2 = bf16[8,128,2048]{2,1,0:T(8,128)(2,1)} async-done(((bf16[8,128,2048]{2,1,0:T(8,128)(2,1)}), bf16[8,128,2048]{2,1,0:T(8,128)(2,1)}, u32[]{:S(2)}, u32[]{:S(2)}) %all-to-all-start.2) | async-done | bytes 4194336 | tf_op jit(solution)/shard_map/all_to_all | solution.py:45
  143.9 4.6 all-to-all-start.1
  148.6 9.3 %fusion.6 = f32[2,8,64,768]{3,2,1,0:T(8,128)} fusion(bf16[2,2048,768]{2,1,0:T(8,128)(2,1)} %param.12, bf16[8,2,64,2048]{3,2,1,0:T(8,128)(2,1)} %bitcast.11), kind=kOutput, calls=%fused_computation.20 | convolution fusion | flops 3221225472 | bytes 13631488 | tf_op jit(solution)/shard_map/sjcd,jdh->sjch/dot_general | solution.py:52
  157.8 84.6 %all-to-all-done.1 = bf16[8,128,2048]{2,1,0:T(8,128)(2,1)} async-done(((bf16[8,128,2048]{2,1,0:T(8,128)(2,1)}), bf16[8,128,2048]{2,1,0:T(8,128)(2,1)}, u32[]{:S(2)}, u32[]{:S(2)}) %all-to-all-start.1) | async-done | bytes 4194336 | tf_op jit(solution)/shard_map/all_to_all | solution.py:46
  242.4 7.5 %fusion.10 = f32[2,8,64,768]{3,2,1,0:T(8,128)S(1)} fusion(bf16[2,2048,768]{2,1,0:T(8,128)(2,1)} %param.14, bf16[8,2,64,2048]{3,2,1,0:T(8,128)(2,1)} %bitcast.49, f32[8,2,64]{2,1,0:T(2,128)S(1)} %reshape.160), kind=kOutput, calls=%fused_computation.24 | convolution fusion | flops 3227516928 | bytes 13635584 | tf_op jit(solution)/shard_map/sjcd,jdh->sjch/dot_general | solution.py:63
  250.0 7.9 %fusion.41 = (bf16[8,2,64,768]{3,2,0,1:T(8,128)(2,1)S(1)}, bf16[8,2,64,768]{3,2,0,1:T(8,128)(2,1)}, bf16[8,2,64,768]{3,2,0,1:T(8,128)(2,1)S(1)}) fusion(f32[2,8,64,768]{3,2,1,0:T(8,128)S(1)} %copy-done.9, f32[2,8,64,768]{3,2,1,0:T(8,128)S(1)} %fusion.10, bf16[2,2048,768]{2,1,0:T(8,128)(2,1)S(1)} %bitcast.166, bf16[8,2,64,2048]{3,2,1,0:T(8,128)(2,1)} %bitcast.11), kind=kOutput, calls=%fused_computation.67 | convolution fusion | flops 3233021952 | bytes 21495808 | tf_op jit(solution)/shard_map/sjcd,jdh->sjch/dot_general | solution.py:53
  257.9 7.2 %fusion.3 = bf16[2048,1,2,768]{0,3,2,1:T(8,128)(2,1)S(1)} fusion(bf16[8,2,64,768]{3,2,0,1:T(8,128)(2,1)S(1)} %get-tuple-element.21, bf16[8,2,64,2048]{3,2,1,0:T(8,128)(2,1)} %bitcast.49, f32[8,2,64]{2,1,0:T(2,128)S(1)} %reshape.160), kind=kOutput, calls=%fused_computation.17 | convolution fusion | flops 3230662656 | bytes 12062720 | tf_op jit(solution)/shard_map/sjcd,sjch->djh/dot_general | solution.py:90
  265.2 6.0 %fusion.2 = bf16[2048,1,2,768]{0,3,2,1:T(8,128)(2,1)S(1)} fusion(bf16[8,2,64,768]{3,2,0,1:T(8,128)(2,1)S(1)} %get-tuple-element.23, bf16[8,2,64,2048]{3,2,1,0:T(8,128)(2,1)} %bitcast.11), kind=kOutput, calls=%fused_computation.16 | convolution fusion | flops 3224371200 | bytes 12058624 | tf_op jit(solution)/shard_map/sjcd,sjch->djh/dot_general | solution.py:89
  271.2 5.9 %fusion.1 = bf16[2048,1,2,768]{0,3,2,1:T(8,128)(2,1)S(1)} fusion(bf16[8,2,64,768]{3,2,0,1:T(8,128)(2,1)S(1)} %copy-done.6, bf16[8,2,64,2048]{3,2,1,0:T(8,128)(2,1)} %bitcast.11), kind=kOutput, calls=%fused_computation.15 | convolution fusion | flops 3224371200 | bytes 12058624 | tf_op jit(solution)/shard_map/sjcd,sjch->djh/dot_general | solution.py:88
  277.2 21.0 %pad_maximum_fusion = bf16[2048,3,2,768]{0,3,2,1:T(8,128)(2,1)} fusion(bf16[2048,1,2,768]{0,3,2,1:T(8,128)(2,1)S(1)} %fusion.3, bf16[2048,1,2,768]{0,3,2,1:T(8,128)(2,1)S(1)} %fusion.2, bf16[2048,1,2,768]{0,3,2,1:T(8,128)(2,1)S(1)} %fusion.1), kind=kLoop, calls=%fused_computation.7 | loop fusion | flops 18874368 | bytes 37748736 | tf_op jit(solution)/shard_map/stack | solution.py:91
  298.2 10.2 %fusion.4 = f32[2,8,64,2048]{3,2,1,0:T(8,128)} fusion(bf16[8,2,64,768]{3,2,0,1:T(8,128)(2,1)} %get-tuple-element.22, bf16[2,2048,768]{2,1,0:T(8,128)(2,1)} %param.12), kind=kOutput, calls=%fused_computation.18 | convolution fusion | flops 3221225472 | bytes 16252928 | tf_op jit(solution)/shard_map/sjch,jdh->sjcd/dot_general | solution.py:67
  308.4 6.5 %fusion.16 = bf16[8,2,64,2048]{3,2,0,1:T(8,128)(2,1)S(1)} fusion(f32[2,8,64,2048]{3,2,1,0:T(8,128)} %fusion.4, bf16[8,2,64,768]{3,2,0,1:T(8,128)(2,1)} %copy-done.5, bf16[2,2048,768]{2,1,0:T(8,128)(2,1)S(1)} %bitcast.168), kind=kOutput, calls=%fused_computation.30 | convolution fusion | flops 3225419776 | bytes 20447232 | tf_op jit(solution)/shard_map/sjch,jdh->sjcd/dot_general | solution.py:68
  317.5 4.8 all-to-all-start.3
  322.3 6.8 %convert_bitcast_fusion.1 = bf16[8,2,64,2048]{3,2,0,1:T(8,128)(2,1)S(1)} fusion(bf16[8,2,64,768]{3,2,0,1:T(8,128)(2,1)S(1)} %copy-done.8, bf16[2,2048,768]{2,1,0:T(8,128)(2,1)} %param.14), kind=kOutput, calls=%fused_computation.34 | convolution fusion | flops 3223322624 | bytes 12058624 | tf_op jit(solution)/shard_map/sjch,jdh->sjcd/dot_general | solution.py:57
  331.4 84.9 %all-to-all-done.3 = bf16[8,128,2048]{2,1,0:T(8,128)(2,1)} async-done(((bf16[8,128,2048]{2,1,0:T(8,128)(2,1)}), bf16[8,128,2048]{2,1,0:T(8,128)(2,1)}, u32[]{:S(2)}, u32[]{:S(2)}) %all-to-all-start.3) | async-done | bytes 4194336 | tf_op jit(solution)/shard_map/all_to_all | solution.py:83
  416.3 4.6 all-to-all-start.4
  433.3 4.9 concatenate.18
  438.2 76.7 %all-to-all-done.4 = bf16[8,128,2048]{2,1,0:T(8,128)(2,1)} async-done(((bf16[8,128,2048]{2,1,0:T(8,128)(2,1)}), bf16[8,128,2048]{2,1,0:T(8,128)(2,1)}, u32[]{:S(2)}, u32[]{:S(2)}) %all-to-all-start.4) | async-done | bytes 4194336 | tf_op jit(solution)/shard_map/all_to_all | solution.py:71
  514.8 4.8 concatenate.19
  519.7 11.6 %gather_fusion.3 = bf16[1024,2048]{1,0:T(8,128)(2,1)} fusion(bf16[1025,2048]{1,0:T(8,128)(2,1)} %concatenate.18, s32[1024]{0:T(1024)S(1)} %broadcast_clamp_fusion), kind=kCustom, calls=%fused_computation.3 | custom fusion | bytes 8392704 | tf_op jit(solution)/shard_map/gather | solution.py:85
  531.2 11.6 %gather_fusion.4 = bf16[1024,2048]{1,0:T(8,128)(2,1)} fusion(bf16[1025,2048]{1,0:T(8,128)(2,1)} %concatenate.19, s32[1024]{0:T(1024)S(1)} %broadcast_clamp_fusion), kind=kCustom, calls=%fused_computation.4 | custom fusion | bytes 8392704 | tf_op jit(solution)/shard_map/gather | solution.py:79
  542.8 5.1 fusion.17
  548.5 5.9 %bitcast_reduce_fusion = bf16[128,2048]{1,0:T(8,128)(2,1)} fusion(bf16[1024,2048]{1,0:T(8,128)(2,1)} %gather_fusion.3), kind=kLoop, calls=%fused_computation.33 | loop fusion | flops 1835008 | bytes 4718592 | tf_op jit(solution)/shard_map/reduce_sum | solution.py:86
  554.4 3.8 convert_bitcast_fusion
  (77 shorter events, 32.5 us)
Async XLA Ops:
  26.7 17.8 %all-to-all-start = ((bf16[8,1,128]{2,1,0:T(2,128)(2,1)}), bf16[8,1,128]{2,1,0:T(2,128)(2,1)S(1)}, u32[]{:S(2)}, u32[]{:S(2)}) async-start(bf16[8,1,128]{2,1,0:T(2,128)(2,1)} %copy.41), calls=%async_computation | async-start | bytes 8192 | tf_op jit(solution)/shard_map/all_to_all | solution.py:47
  44.5 5.2 copy-start.3
  44.5 99.3 %all-to-all-start.2 = ((bf16[8,128,2048]{2,1,0:T(8,128)(2,1)}), bf16[8,128,2048]{2,1,0:T(8,128)(2,1)}, u32[]{:S(2)}, u32[]{:S(2)}) async-start(bf16[8,128,2048]{2,1,0:T(8,128)(2,1)} %bitcast.160), calls=%async_computation.2 | async-start | bytes 8388608 | tf_op jit(solution)/shard_map/all_to_all | solution.py:45
  143.9 98.6 %all-to-all-start.1 = ((bf16[8,128,2048]{2,1,0:T(8,128)(2,1)}), bf16[8,128,2048]{2,1,0:T(8,128)(2,1)}, u32[]{:S(2)}, u32[]{:S(2)}) async-start(bf16[8,128,2048]{2,1,0:T(8,128)(2,1)} %bitcast.159), calls=%async_computation.1 | async-start | bytes 8388608 | tf_op jit(solution)/shard_map/all_to_all | solution.py:46
  148.4 406.0 %reduce-scatter.2.cloned.1.call-start = ((), (), s32[]{:S(2)}) async-start(), calls=%async_computation.6 | async-start | bytes 23592960 | tf_op jit(solution)/shard_map/reduce_scatter | solution.py:92
  148.6 101.4 %slice-start = ((s8[6291456]{0:T(1024)(128)(4,1)}), s8[2097152]{0:T(1024)(128)(4,1)S(1)}, s32[]{:S(2)}) async-start(s8[6291456]{0:T(1024)(128)(4,1)} %bitcast.165), calls=%async_computation.7 | async-start | bytes 4194304
  242.4 7.5 %slice-start.1 = ((s8[6291456]{0:T(1024)(128)(4,1)}), s8[4194304]{0:T(1024)(128)(4,1)S(1)}, s32[]{:S(2)}) async-start(s8[6291456]{0:T(1024)(128)(4,1)} %bitcast.165), calls=%async_computation.8 | async-start | bytes 8388608
  242.4 7.5 %copy-start.9 = (f32[2,8,64,768]{3,2,1,0:T(8,128)S(1)}, f32[2,8,64,768]{3,2,1,0:T(8,128)}, u32[]{:S(2)}) copy-start(f32[2,8,64,768]{3,2,1,0:T(8,128)} %fusion.6) | copy-start | bytes 9437188
  257.9 7.2 %copy-start.7 = (bf16[8,2,64,768]{3,2,0,1:T(8,128)(2,1)}, bf16[8,2,64,768]{3,2,0,1:T(8,128)(2,1)S(1)}, u32[]{:S(2)}) copy-start(bf16[8,2,64,768]{3,2,0,1:T(8,128)(2,1)S(1)} %get-tuple-element.21) | copy-start | bytes 4718596
  257.9 7.3 %copy-start.5 = (bf16[8,2,64,768]{3,2,0,1:T(8,128)(2,1)}, bf16[8,2,64,768]{3,2,0,1:T(8,128)(2,1)S(1)}, u32[]{:S(2)}) copy-start(bf16[8,2,64,768]{3,2,0,1:T(8,128)(2,1)S(1)} %get-tuple-element.23) | copy-start | bytes 4718596
  265.1 6.1 %copy-start.6 = (bf16[8,2,64,768]{3,2,0,1:T(8,128)(2,1)S(1)}, bf16[8,2,64,768]{3,2,0,1:T(8,128)(2,1)}, u32[]{:S(2)}) copy-start(bf16[8,2,64,768]{3,2,0,1:T(8,128)(2,1)} %get-tuple-element.22) | copy-start | bytes 4718596
  298.1 10.2 %slice-start.2 = ((s8[6291456]{0:T(1024)(128)(4,1)}), s8[2097152]{0:T(1024)(128)(4,1)S(1)}, s32[]{:S(2)}) async-start(s8[6291456]{0:T(1024)(128)(4,1)} %bitcast.167), calls=%async_computation.9 | async-start | bytes 4194304
  298.2 10.2 %slice-start.3 = ((s8[6291456]{0:T(1024)(128)(4,1)}), s8[4194304]{0:T(1024)(128)(4,1)S(1)}, s32[]{:S(2)}) async-start(s8[6291456]{0:T(1024)(128)(4,1)} %bitcast.167), calls=%async_computation.10 | async-start | bytes 8388608
  317.5 4.8 copy-start.8
  317.5 98.8 %all-to-all-start.3 = ((bf16[8,128,2048]{2,1,0:T(8,128)(2,1)}), bf16[8,128,2048]{2,1,0:T(8,128)(2,1)}, u32[]{:S(2)}, u32[]{:S(2)}) async-start(bf16[8,128,2048]{2,1,0:T(8,128)(2,1)} %bitcast.162), calls=%async_computation.3 | async-start | bytes 8388608 | tf_op jit(solution)/shard_map/all_to_all | solution.py:83
  416.3 98.6 %all-to-all-start.4 = ((bf16[8,128,2048]{2,1,0:T(8,128)(2,1)}), bf16[8,128,2048]{2,1,0:T(8,128)(2,1)}, u32[]{:S(2)}, u32[]{:S(2)}) async-start(bf16[8,128,2048]{2,1,0:T(8,128)(2,1)} %bitcast.161), calls=%async_computation.4 | async-start | bytes 8388608 | tf_op jit(solution)/shard_map/all_to_all | solution.py:71
  420.8 2.3 copy-start.4
  554.4 3.8 copy-start
  561.8 2.7 copy-start.2
  561.8 4.3 copy-start.1
Sparse Core Ops, SparseCore 0:
  298.3 169.6 reduce-scatter.1
where the time goes:
time: 575 us
  waiting for transfers between devices  334 us (58%)
  local copies, waits for them, and re-layouts  88.2 us (15%)
  matrix products  72.3 us (13%)
  other arithmetic  39.8 us (7%)
  starting transfers between devices  25.5 us (4%)
  between operations  14.6 us (3%)
    all_to_all x1, waiting for transfers between devices, body(): lax.all_to_all(send_x, 'expert', split_axis=0, concat_axis=0, tiled=True)  88 us
    all_to_all x1, waiting for transfers between devices, body(): lax.all_to_all(dx_send, 'expert', split_axis=0, concat_axis=0, tiled=True)  84.9 us
    all_to_all x1, waiting for transfers between devices, body(): lax.all_to_all(send_dy, 'expert', split_axis=0, concat_axis=0, tiled=True)  84.6 us
    all_to_all x1, waiting for transfers between devices, body(): lax.all_to_all(outs.reshape(n_owner, local_exp * capacity, width), 'exper...  76.7 us
    another operation x1, other arithmetic, body(): stacked = jnp.stack([grad_g, grad_u, grad_d], axis=1)  21 us
    unnamed x36, local copies, waits for them, and re-layouts  12.6 us
    gather x1, local copies, waits for them, and re-layouts, body(): routed_out = out_pad[slots].reshape(tok_rows, topk, width)  11.6 us
    gather x1, local copies, waits for them, and re-layouts, body(): routed_dx = dx_pad[slots].reshape(tok_rows, topk, width)  11.6 us
  transfers between devices with their start and end apart: 6, of which 4 were waited for; matrix products, arithmetic and copies ran while one was open for 20% of the time, Pallas kernels for 0%

commit v1 on v0

v1 whole, which is shorter than its diff:
```python
import jax
import jax.numpy as jnp
from jax import lax
from jax.sharding import PartitionSpec as P

step_size = 0.004
shrink_rate = 0.1
F32 = jnp.float32
BF16 = jnp.bfloat16


def mm(spec, a, b, out=F32):
    r = jnp.einsum(spec, a, b, preferred_element_type=F32)
    return r if out == F32 else r.astype(out)


def body(tokens, out_grad, expert_ids, route_probs, w_gate, w_up, w_down, decay_mask):
    n_owner = lax.axis_size("expert")
    n_group = lax.axis_size("dp")
    local_exp = w_gate.shape[0]
    width = tokens.shape[1]
    hidden = w_gate.shape[2]
    tok_rows = tokens.shape[0]
    topk = expert_ids.shape[1]
    n_experts = n_owner * local_exp
    capacity = tok_rows * topk // n_experts
    me_q = lax.axis_index("expert")
    me_p = lax.axis_index("dp")
    lo = me_p % 2
    hi = me_p // 2
    shard_rows = width // n_group

    meta = jnp.concatenate([expert_ids.astype(BF16), route_probs], axis=1)
    all_meta = lax.all_gather(meta, "expert", axis=0, tiled=True)
    x_all = lax.all_gather(tokens, "expert", axis=0, tiled=True)
    dy_all = lax.all_gather(out_grad, "expert", axis=0, tiled=True)

    meta_b = all_meta.reshape(n_owner, tok_rows, 2 * topk).astype(F32)
    ids_b = meta_b[..., :topk].astype(jnp.int32)
    probs_b = meta_b[..., topk:]
    mine = me_q * local_exp + jnp.arange(local_exp, dtype=jnp.int32)
    hit = ids_b[:, None, :, :] == mine[None, :, None, None]
    picked = jnp.any(hit, axis=3)
    p_tok = jnp.sum(jnp.where(hit, probs_b[:, None], 0.0), axis=3)
    earlier = (
        jnp.arange(tok_rows)[:, None] < jnp.arange(tok_rows)[None, :]
    ).astype(BF16)
    position = mm("bes,st->bet", picked.astype(BF16), earlier).astype(jnp.int32)
    spot = jnp.where(picked, position, capacity)
    disp_bool = spot[:, :, None, :] == jnp.arange(capacity)[None, None, :, None]
    disp = disp_bool.astype(BF16)
    p_slot = jnp.sum(jnp.where(disp_bool, p_tok[:, :, None, :], 0.0), axis=3)
    p_slot = p_slot.transpose(1, 0, 2).reshape(local_exp, n_owner * capacity)
    slots = n_owner * capacity

    x_b = x_all.reshape(n_owner, tok_rows, width)
    rows_x = mm("bect,btd->ebcd", disp, x_b, BF16).reshape(local_exp, slots, width)
    gate = mm("erd,edh->erh", rows_x, w_gate)
    upper = mm("erd,edh->erh", rows_x, w_up)
    sig = jax.nn.sigmoid(gate)
    act = gate * sig
    hid_f = act * upper
    hid_p = (hid_f * p_slot[..., None]).astype(BF16)
    dact = upper * sig * (1.0 + gate * (1.0 - sig))

    dy_b = dy_all.reshape(n_owner, tok_rows, width)
    rows_dy = mm("bect,btd->ebcd", disp, dy_b, BF16).reshape(local_exp, slots, width)

    def pick(rows, axis_bit, which):
        v = rows.reshape(slots, 2, 2, shard_rows)
        axis = 2 if axis_bit == 1 else 1
        return lax.dynamic_index_in_dim(v, which, axis, keepdims=False)

    def swap(v, bit):
        return lax.ppermute(v, "dp", [(i, i ^ bit) for i in range(n_group)])

    def reduce_rows(left, right, bit):
        first, second = (lo, hi) if bit == 1 else (hi, lo)
        out = mm("rad,rh->adh", pick(left, bit, 1 - first), right, BF16)
        got = swap(out, bit)
        keep = mm("rad,rh->adh", pick(left, bit, first), right, BF16)
        half = keep.astype(F32) + got.astype(F32)
        own = lax.dynamic_index_in_dim(half, second, 0, keepdims=False)
        away = lax.dynamic_index_in_dim(half, 1 - second, 0, keepdims=False).astype(BF16)
        return own + swap(away, 3 - bit).astype(F32)

    bits = [1 + (e % 2) for e in range(local_exp)]
    g_down = [reduce_rows(rows_dy[e], hid_p[e], bits[e]) for e in range(local_exp)]

    u = mm("erd,edh->erh", rows_dy, w_down)
    dprob_slot = jnp.sum(u * hid_f.astype(BF16).astype(F32), axis=2)
    dhid = u * p_slot[..., None]
    dgate = (dhid * dact).astype(BF16)
    dup = (dhid * act).astype(BF16)
    g_gate = [reduce_rows(rows_x[e], dgate[e], bits[e]) for e in range(local_exp)]
    g_up = [reduce_rows(rows_x[e], dup[e], bits[e]) for e in range(local_exp)]

    dx = (mm("erh,edh->erd", dgate, w_gate) + mm("erh,edh->erd", dup, w_up)).astype(BF16)
    part = mm(
        "bect,ebcd->btd", disp, dx.reshape(local_exp, n_owner, capacity, width), BF16
    ).reshape(n_owner * tok_rows, width)
    grad_tokens = lax.psum_scatter(part, "expert", scatter_dimension=0, tiled=True)

    dprob = dprob_slot.reshape(local_exp, n_owner, capacity).transpose(1, 0, 2)
    q_tok = jnp.sum(jnp.where(disp_bool, dprob[..., None], 0.0), axis=2)
    q_got = lax.all_to_all(q_tok.astype(BF16), "expert", split_axis=0, concat_axis=0, tiled=True)
    q_got = q_got.reshape(n_experts, tok_rows).astype(F32)
    sel = expert_ids[:, :, None] == jnp.arange(n_experts, dtype=jnp.int32)[None, None, :]
    grad_probs = jnp.sum(jnp.where(sel, q_got.T[:, None, :], 0.0), axis=2).astype(BF16)

    rates = decay_mask.astype(F32)

    def update(weight, grads, column):
        own = lax.dynamic_slice_in_dim(weight, me_p * shard_rows, shard_rows, 1).astype(F32)
        factor = rates[:, column][:, None, None]
        return (own - step_size * jnp.stack(grads) - shrink_rate * factor * own).astype(BF16)

    return (
        grad_tokens,
        grad_probs,
        update(w_gate, g_gate, 0),
        update(w_up, g_up, 1),
        update(w_down, g_down, 2),
    )


def solution(mesh):
    placed = (
        P(("dp", "expert"), None),
        P(("dp", "expert"), None),
        P(("dp", "expert"), None),
        P(("dp", "expert"), None),
        P("expert", None, None),
        P("expert", None, None),
        P("expert", None, None),
        P("expert", None),
    )
    return jax.shard_map(
        body,
        mesh=mesh,
        in_specs=placed,
        out_specs=(
            P(("dp", "expert"), None),
            P(("dp", "expert"), None),
            P("expert", "dp", None),
            P("expert", "dp", None),
            P("expert", "dp", None),
        ),
        check_vma=False,
    )
```

time: 575 us -> 418 us (0.73)
  waiting for transfers between devices: 334 us -> 198 us
  other arithmetic: 39.8 us -> 20.5 us
  local copies, waits for them, and re-layouts: 88.2 us -> 73.1 us
  blocking collectives: 0 us -> 14.5 us
  starting transfers between devices: 25.5 us -> 15.6 us
    all_to_all x5 -> x1, waiting for transfers between devices: 334 us -> 0.01 us  [body(): lax.all_to_all(q_tok.astype(BF16), 'expert', split_axis=0, concat_axis=0,...]
    ppermute x0 -> x12, waiting for transfers between devices: none -> 124 us  [swap(): return lax.ppermute(v, 'dp', [(i, i ^ bit) for i in range(n_group)])]
    all_gather x0 -> x2, waiting for transfers between devices: none -> 73.2 us  [the longest x1 39.5 us: body(): x_all = lax.all_gather(tokens, 'expert', axis=0, tiled=True)]
    gather x5 -> x0, local copies, waits for them, and re-layouts: 42 us -> none  [the longest x1 11.6 us: body(): routed_out = out_pad[slots].reshape(tok_rows, topk, width)]
    dynamic_slice x3 -> x10, local copies, waits for them, and re-layouts: 7.08 us -> 46.1 us  [pick(): return lax.dynamic_index_in_dim(v, which, axis, keepdims=False)]
    another operation x4 -> x6, other arithmetic: 25.6 us -> 0.95 us  [update(): jnp.stack(grads)]
    all_to_all x5 -> x1, starting transfers between devices: 25.4 us -> 3.29 us  [body(): lax.all_to_all(q_tok.astype(BF16), 'expert', split_axis=0, concat_axis=0,...]
    another operation x2 -> x4, local copies, waits for them, and re-layouts: 0.08 us -> 16.9 us  [pick(): v = rows.reshape(slots, 2, 2, shard_rows)]
  transfers between devices with their start and end apart: 6 -> 16, of which waited for: 4 -> 9; matrix products, arithmetic and copies ran while one was open for 20% -> 27% of each run, Pallas kernels for 0% -> 0%
where the time goes in v1:
time: 418 us; the launch traced here: 413 us
  waiting for transfers between devices  198 us (47%)
  matrix products  76.7 us (18%)
  local copies, waits for them, and re-layouts  73.1 us (17%)
  other arithmetic  20.5 us (5%)
  starting transfers between devices  15.6 us (4%)
  between operations  14.7 us (4%)
  blocking collectives  14.5 us (3%)
    ppermute x12, waiting for transfers between devices, swap(): return lax.ppermute(v, 'dp', [(i, i ^ bit) for i in range(n_group)])  124 us
    dot_general x21, matrix products, mm(): r = jnp.einsum(spec, a, b, preferred_element_type=F32)  76.7 us
    dynamic_slice x10, local copies, waits for them, and re-layouts, pick(): return lax.dynamic_index_in_dim(v, which, axis, keepdims=False)  46.1 us
    all_gather x1, waiting for transfers between devices, body(): x_all = lax.all_gather(tokens, 'expert', axis=0, tiled=True)  39.5 us
    all_gather x1, waiting for transfers between devices, body(): dy_all = lax.all_gather(out_grad, 'expert', axis=0, tiled=True)  33.6 us
    another operation x4, local copies, waits for them, and re-layouts, pick(): v = rows.reshape(slots, 2, 2, shard_rows)  16.9 us
    all_gather x1, blocking collectives, body(): all_meta = lax.all_gather(meta, 'expert', axis=0, tiled=True)  14.5 us
    ppermute x12, starting transfers between devices, swap(): return lax.ppermute(v, 'dp', [(i, i ^ bit) for i in range(n_group)])  12.2 us
  transfers between devices with their start and end apart: 16, of which 9 were waited for; matrix products, arithmetic and copies ran while one was open for 27% of the time, Pallas kernels for 0%

profile of v1, /device:TPU:0, one launch (start us, length us, event | category | flops | bytes accessed | tf_op | source)
XLA Modules:
  0.0 413.2 jit_solution(4033411544377260447)
XLA Ops:
  10.7 14.5 %all_gather.9 = bf16[1024,16]{0,1:T(8,128)(2,1)S(1)} all-gather(bf16[128,16]{0,1:T(8,128)(2,1)S(1)} %pad_maximum_fusion), channel_id=1, replica_groups=mesh['dp'=4,'expert'=8] {'expert'}, dimensions={0}, use_global_device_ids=true | all-gather | bytes 36864 | tf_op jit(solution)/shard_map/all_gather | solution.py:34
  25.9 33.6 %all-gather.3.cloned.1.call-done = bf16[1024,2048]{1,0:T(8,128)(2,1)} async-done(((bf16[128,2048]{1,0:T(8,128)(2,1)}), bf16[1024,2048]{1,0:T(8,128)(2,1)}) %all-gather.3.cloned.1.call-update) | async-done | bytes 4194320 | tf_op jit(solution)/shard_map/all_gather | solution.py:36
  59.5 3.4 convert_bitcast_fusion.1
  67.6 39.5 %all-gather.5.cloned.1.call-done = bf16[1024,2048]{1,0:T(8,128)(2,1)} async-done(((bf16[128,2048]{1,0:T(8,128)(2,1)}), bf16[1024,2048]{1,0:T(8,128)(2,1)}) %all-gather.5.cloned.1.call-update) | async-done | bytes 4194320 | tf_op jit(solution)/shard_map/all_gather | solution.py:35
  107.2 3.4 convert_bitcast_fusion
  115.2 3.4 reshape_squeeze.10
  118.6 4.5 %reshape_squeeze.11 = bf16[512,2,2,512]{3,2,1,0:T(2,128)(2,1)} reshape(bf16[1,8,64,2048]{3,2,0,1:T(8,128)(2,1)} %get-tuple-element.14) | data formatting | bytes 4194304 | tf_op jit(solution)/shard_map/reshape;squeeze | solution.py:70
  123.1 4.5 %reshape_squeeze.8 = bf16[512,2,2,512]{3,2,1,0:T(2,128)(2,1)} reshape(bf16[1,8,64,2048]{3,2,0,1:T(8,128)(2,1)} %get-tuple-element.15) | data formatting | bytes 4194304 | tf_op jit(solution)/shard_map/reshape;squeeze | solution.py:70
  127.6 4.5 %reshape_squeeze.9 = bf16[512,2,2,512]{3,2,1,0:T(2,128)(2,1)} reshape(bf16[1,8,64,2048]{3,2,0,1:T(8,128)(2,1)} %get-tuple-element.16) | data formatting | bytes 4194304 | tf_op jit(solution)/shard_map/reshape;squeeze | solution.py:70
  132.1 5.4 %constant_dynamic-slice_fusion.1 = (bf16[512,1,2,512]{3,2,1,0:T(2,128)(2,1)}, bf16[512,1,2,512]{3,2,1,0:T(2,128)(2,1)}, bf16[512,1,2,512]{3,2,1,0:T(2,128)(2,1)}, bf16[512,1,2,512]{3,2,1,0:T(2,128)(2,1)S(1)}) fusion(bf16[512,2,2,512]{3,2,1,0:T(2,128)(2,1)} %reshape_squeeze.11, s32[]{:T(128)S(6)} %select_n.81, s32[]{:T(128)S(6)} %select_n.82, ...), kind=kLoop, calls=%fused_computation.106 | loop fusion | bytes 8388616 | tf_op jit(solution)/shard_map/jit(dynamic_index_in_dim)/dynamic_slice | solution.py:72
  137.5 3.7 copy.91
  141.2 3.7 copy.95
  144.9 7.2 %fusion.44 = f32[2,512,768]{2,1,0:T(8,128)S(1)} fusion(bf16[2,512,2048]{2,1,0:T(8,128)(2,1)} %bitcast.178, bf16[2,2048,768]{2,1,0:T(8,128)(2,1)} %param.12), kind=kOutput, calls=%fused_computation.122 | convolution fusion | flops 3221225472 | bytes 13631488 | tf_op jit(solution)/shard_map/erd,edh->erh/dot_general | solution.py:13
  152.1 6.7 %fusion.43 = f32[2,512,768]{2,1,0:T(8,128)S(1)} fusion(bf16[2,512,2048]{2,1,0:T(8,128)(2,1)S(1)} %bitcast.179, bf16[2,2048,768]{2,1,0:T(8,128)(2,1)} %param.13), kind=kOutput, calls=%fused_computation.121 | convolution fusion | flops 3221225472 | bytes 13631488 | tf_op jit(solution)/shard_map/erd,edh->erh/dot_general | solution.py:13
  158.8 5.4 %multiply_reduce_fusion = (f32[2,512]{1,0:T(2,128)S(1)}, f32[2,512,768]{2,1,0:T(8,128)}) fusion(f32[2,512,768]{2,1,0:T(8,128)S(1)} %fusion.43, f32[2,512,768]{2,1,0:T(8,128)S(1)} %fusion.44, bf16[2,512,2048]{2,1,0:T(8,128)(2,1)S(1)} %bitcast.177, bf16[2,2048,768]{2,1,0:T(8,128)(2,1)S(1)} %bitcast.181), kind=kOutput, calls=%fused_computation.27 | convolution fusion | flops 3228302336 | bytes 19927040 | tf_op jit(solution)/shard_map/erd,edh->erh/dot_general | solution.py:13
  168.6 5.8 %multiply_convert_fusion = (bf16[2,512,768]{2,1,0:T(8,128)(2,1)}, bf16[2,512,768]{2,1,0:T(8,128)(2,1)S(1)}, bf16[2,512,768]{2,1,0:T(8,128)(2,1)S(1)}) fusion(f32[2,512]{1,0:T(2,128)S(1)} %mul.115, f32[2,512,768]{2,1,0:T(8,128)} %copy-done.14, f32[2,512,768]{2,1,0:T(8,128)} %copy-done.13, f32[2,512,768]{2,1,0:T(8,128)} %get-tuple-element.28), kind=kLoop, calls=%fused_computation.22 | loop fusion | flops 13369344 | bytes 14159872 | tf_op jit(solution)/shard_map/convert_element_type | solution.py:63
  178.2 8.4 %fusion.45 = f32[2,512,2048]{2,1,0:T(8,128)} fusion(bf16[2,512,768]{2,1,0:T(8,128)(2,1)S(1)} %get-tuple-element.11, bf16[2,2048,768]{2,1,0:T(8,128)(2,1)} %param.12), kind=kOutput, calls=%fused_computation.123 | convolution fusion | flops 3221225472 | bytes 16252928 | tf_op jit(solution)/shard_map/erh,edh->erd/dot_general | solution.py:13
  186.6 7.8 %add_convert_fusion = bf16[2,512,2048]{2,1,0:T(8,128)(2,1)S(1)} fusion(f32[2,512,2048]{2,1,0:T(8,128)} %fusion.45, bf16[2,512,768]{2,1,0:T(8,128)(2,1)S(1)} %get-tuple-element.12, bf16[2,2048,768]{2,1,0:T(8,128)(2,1)} %param.13), kind=kOutput, calls=%fused_computation.1 | convolution fusion | flops 3225419776 | bytes 20447232 | tf_op jit(solution)/shard_map/erh,edh->erd/dot_general | solution.py:13
  197.7 3.7 convolution_convert_fusion.8
  205.6 9.8 %constant_dynamic-slice_fusion.3 = (bf16[512,2,1,512]{3,2,1,0:T(2,128)(2,1)}, bf16[512,2,1,512]{3,2,1,0:T(2,128)(2,1)}, bf16[512,2,1,512]{3,2,1,0:T(2,128)(2,1)}, bf16[512,2,1,512]{3,2,1,0:T(2,128)(2,1)}) fusion(bf16[512,2,2,512]{3,2,1,0:T(2,128)(2,1)S(1)} %reshape_squeeze.10, s32[]{:T(128)S(6)} %select_n.78, s32[]{:T(128)S(6)} %select_n.79, ...), kind=kLoop, calls=%fused_computation.108 | loop fusion | bytes 8388616 | tf_op jit(solution)/shard_map/jit(dynamic_index_in_dim)/dynamic_slice | solution.py:72
  215.5 6.0 %copy.89 = bf16[512,2,1,512]{0,3,1,2:T(8,128)(2,1)} copy(bf16[512,2,1,512]{3,2,1,0:T(2,128)(2,1)} %get-tuple-element.31) | data formatting | bytes 2097152 | tf_op jit(solution)/shard_map/jit(dynamic_index_in_dim)/dynamic_slice | solution.py:72
  221.5 3.6 convolution_convert_fusion.6
  225.1 4.4 %copy.93 = bf16[512,2,1,512]{0,3,1,2:T(8,128)(2,1)} copy(bf16[512,2,1,512]{3,2,1,0:T(2,128)(2,1)S(1)} %copy-done.1) | data formatting | bytes 2097152 | tf_op jit(solution)/shard_map/jit(dynamic_index_in_dim)/dynamic_slice | solution.py:72
  229.5 3.8 convolution_convert_fusion.10
  239.4 4.6 %copy.92 = bf16[512,2,1,512]{0,3,1,2:T(8,128)(2,1)S(1)} copy(bf16[512,2,1,512]{3,2,1,0:T(2,128)(2,1)} %get-tuple-element.17) | data formatting | bytes 2097152 | tf_op jit(solution)/shard_map/jit(dynamic_index_in_dim)/dynamic_slice | solution.py:72
  244.0 4.6 %copy.88 = bf16[512,2,1,512]{0,3,1,2:T(8,128)(2,1)S(1)} copy(bf16[512,2,1,512]{3,2,1,0:T(2,128)(2,1)} %get-tuple-element.32) | data formatting | bytes 2097152 | tf_op jit(solution)/shard_map/jit(dynamic_index_in_dim)/dynamic_slice | solution.py:72
  258.8 22.3 %collective-permute-done.10 = bf16[2,512,768]{2,1,0:T(8,128)(2,1)} collective-permute-done((bf16[2,512,768]{2,1,0:T(8,128)(2,1)}, bf16[2,512,768]{2,1,0:T(8,128)(2,1)}, u32[]{:S(2)}, u32[]{:S(2)}) %collective-permute-start.10) | collective-permute-done | bytes 1572896 | tf_op jit(solution)/shard_map/ppermute | solution.py:75
  290.3 29.7 %collective-permute-done.4 = bf16[2,512,768]{2,1,0:T(8,128)(2,1)} collective-permute-done((bf16[2,512,768]{2,1,0:T(8,128)(2,1)}, bf16[2,512,768]{2,1,0:T(8,128)(2,1)}, u32[]{:S(2)}, u32[]{:S(2)}) %collective-permute-start.4) | collective-permute-done | bytes 1572896 | tf_op jit(solution)/shard_map/ppermute | solution.py:75
  323.0 30.6 %collective-permute-done.8 = bf16[2,512,768]{2,1,0:T(8,128)(2,1)S(1)} collective-permute-done((bf16[2,512,768]{2,1,0:T(8,128)(2,1)}, bf16[2,512,768]{2,1,0:T(8,128)(2,1)S(1)}, u32[]{:S(2)}, u32[]{:S(2)}) %collective-permute-start.8) | collective-permute-done | bytes 1572896 | tf_op jit(solution)/shard_map/ppermute | solution.py:75
  355.2 15.2 %collective-permute-done.7 = bf16[512,768]{1,0:T(8,128)(2,1)S(1)} collective-permute-done((bf16[512,768]{1,0:T(8,128)(2,1)S(1)}, bf16[512,768]{1,0:T(8,128)(2,1)S(1)}, u32[]{:S(2)}, u32[]{:S(2)}) %collective-permute-start.7) | collective-permute-done | bytes 786464 | tf_op jit(solution)/shard_map/ppermute | solution.py:75
  371.2 16.2 %collective-permute-done.3 = bf16[512,768]{1,0:T(8,128)(2,1)S(1)} collective-permute-done((bf16[512,768]{1,0:T(8,128)(2,1)S(1)}, bf16[512,768]{1,0:T(8,128)(2,1)S(1)}, u32[]{:S(2)}, u32[]{:S(2)}) %collective-permute-start.3) | collective-permute-done | bytes 786464 | tf_op jit(solution)/shard_map/ppermute | solution.py:75
  394.4 8.3 %collective-permute-done.11 = bf16[512,768]{1,0:T(8,128)(2,1)S(1)} collective-permute-done((bf16[512,768]{1,0:T(8,128)(2,1)S(1)}, bf16[512,768]{1,0:T(8,128)(2,1)S(1)}, u32[]{:S(2)}, u32[]{:S(2)}) %collective-permute-start.11) | collective-permute-done | bytes 786464 | tf_op jit(solution)/shard_map/ppermute | solution.py:75
  (122 shorter events, 70.3 us)
Async XLA Ops:
  7.2 52.4 %all-gather.3.cloned.1.call-start = ((), (), s32[]{:S(2)}) async-start(), calls=%async_computation.2 | async-start | bytes 4718592 | tf_op jit(solution)/shard_map/all_gather | solution.py:36
  7.9 99.3 %all-gather.5.cloned.1.call-start = ((), (), s32[]{:S(2)}) async-start(), calls=%async_computation.3 | async-start | bytes 4718592 | tf_op jit(solution)/shard_map/all_gather | solution.py:35
  144.8 7.2 %copy-start.12 = (bf16[2,8,64,2048]{3,2,1,0:T(8,128)(2,1)S(1)}, bf16[2,8,64,2048]{3,2,1,0:T(8,128)(2,1)}, u32[]{:S(2)}) copy-start(bf16[2,8,64,2048]{3,2,1,0:T(8,128)(2,1)} %copy.85) | copy-start | bytes 12582916
  144.8 13.9 %slice-start = ((s8[6291456]{0:T(1024)(128)(4,1)}), s8[4194304]{0:T(1024)(128)(4,1)S(1)}, s32[]{:S(2)}) async-start(s8[6291456]{0:T(1024)(128)(4,1)} %bitcast.180), calls=%async_computation.5 | async-start | bytes 8388608
  152.0 6.7 %copy-start.13 = (f32[2,512,768]{2,1,0:T(8,128)}, f32[2,512,768]{2,1,0:T(8,128)S(1)}, u32[]{:S(2)}) copy-start(f32[2,512,768]{2,1,0:T(8,128)S(1)} %fusion.44) | copy-start | bytes 9437188
  152.1 6.7 %copy-start.11 = (bf16[2,8,64,2048]{3,2,1,0:T(8,128)(2,1)S(1)}, bf16[2,8,64,2048]{3,2,1,0:T(8,128)(2,1)}, u32[]{:S(2)}) copy-start(bf16[2,8,64,2048]{3,2,1,0:T(8,128)(2,1)} %copy.82) | copy-start | bytes 12582916
  152.1 6.7 %slice-start.1 = ((s8[6291456]{0:T(1024)(128)(4,1)}), s8[2097152]{0:T(1024)(128)(4,1)S(1)}, s32[]{:S(2)}) async-start(s8[6291456]{0:T(1024)(128)(4,1)} %bitcast.180), calls=%async_computation.6 | async-start | bytes 4194304
  158.8 5.5 %copy-start.14 = (f32[2,512,768]{2,1,0:T(8,128)}, f32[2,512,768]{2,1,0:T(8,128)S(1)}, u32[]{:S(2)}) copy-start(f32[2,512,768]{2,1,0:T(8,128)S(1)} %fusion.43) | copy-start | bytes 9437188
  165.3 85.4 %all-to-all-start = ((bf16[8,2,128]{2,1,0:T(2,128)(2,1)}), bf16[8,2,128]{2,1,0:T(2,128)(2,1)S(1)}, u32[]{:S(2)}, u32[]{:S(2)}) async-start(bf16[8,2,128]{2,1,0:T(2,128)(2,1)} %get-tuple-element.5), calls=%async_computation.1 | async-start | bytes 8192 | tf_op jit(solution)/shard_map/all_to_all | solution.py:106
  168.5 237.7 %reduce-scatter.2.cloned.1.call-start = ((), (), s32[]{:S(2)}) async-start(), calls=%async_computation.4 | async-start | bytes 4718592 | tf_op jit(solution)/shard_map/reduce_scatter | solution.py:102
  168.6 5.8 %copy-start.17 = (bf16[512,1,2,512]{0,3,2,1:T(8,128)(2,1)S(1)}, bf16[512,1,2,512]{0,3,2,1:T(8,128)(2,1)}, u32[]{:S(2)}) copy-start(bf16[512,1,2,512]{0,3,2,1:T(8,128)(2,1)} %copy.91) | copy-start | bytes 3145732
  174.4 12.2 %copy-start.5 = (bf16[2,512,768]{2,1,0:T(8,128)(2,1)}, bf16[2,512,768]{2,1,0:T(8,128)(2,1)S(1)}, u32[]{:S(2)}) copy-start(bf16[2,512,768]{2,1,0:T(8,128)(2,1)S(1)} %get-tuple-element.12) | copy-start | bytes 4718596
  174.4 12.2 %copy-start.7 = (bf16[2,512,768]{2,1,0:T(8,128)(2,1)}, bf16[2,512,768]{2,1,0:T(8,128)(2,1)S(1)}, u32[]{:S(2)}) copy-start(bf16[2,512,768]{2,1,0:T(8,128)(2,1)S(1)} %get-tuple-element.11) | copy-start | bytes 4718596
  176.7 74.6 %collective-permute-start.6 = (bf16[2,512,768]{2,1,0:T(8,128)(2,1)}, bf16[2,512,768]{2,1,0:T(8,128)(2,1)}, u32[]{:S(2)}, u32[]{:S(2)}) collective-permute-start(bf16[2,512,768]{2,1,0:T(8,128)(2,1)} %convolution_convert_fusion.4), channel_id=1, source_target_pairs={{0,16},{8,24},{16,0},{24,8},{1,17},{9,25},{17,1},{25,9},{2,18},{10... | collective-permute-start | bytes 4718600 | tf_op jit(solution)/shard_map/ppermute | solution.py:75
  197.7 4.3 %copy-start.2 = (bf16[2,512,768]{2,1,0:T(8,128)(2,1)S(1)}, bf16[2,512,768]{2,1,0:T(8,128)(2,1)}, u32[]{:S(2)}) copy-start(bf16[2,512,768]{2,1,0:T(8,128)(2,1)} %get-tuple-element.10) | copy-start | bytes 4718596
  201.5 54.1 %collective-permute-start.2 = (bf16[2,512,768]{2,1,0:T(8,128)(2,1)}, bf16[2,512,768]{2,1,0:T(8,128)(2,1)}, u32[]{:S(2)}, u32[]{:S(2)}) collective-permute-start(bf16[2,512,768]{2,1,0:T(8,128)(2,1)} %convolution_convert_fusion.8), channel_id=1, source_target_pairs={{0,16},{8,24},{16,0},{24,8},{1,17},{9,25},{17,1},{25,9},{2,18},{10... | collective-permute-start | bytes 4718600 | tf_op jit(solution)/shard_map/ppermute | solution.py:75
  204.2 76.9 %collective-permute-start.10 = (bf16[2,512,768]{2,1,0:T(8,128)(2,1)}, bf16[2,512,768]{2,1,0:T(8,128)(2,1)}, u32[]{:S(2)}, u32[]{:S(2)}) collective-permute-start(bf16[2,512,768]{2,1,0:T(8,128)(2,1)} %convolution_convert_fusion), channel_id=1, source_target_pairs={{0,16},{8,24},{16,0},{24,8},{1,17},{9,25},{17,1},{25,9},{2,18},{10... | collective-permute-start | bytes 4718600 | tf_op jit(solution)/shard_map/ppermute | solution.py:75
  215.5 9.6 %copy-start.1 = (bf16[512,2,1,512]{3,2,1,0:T(2,128)(2,1)S(1)}, bf16[512,2,1,512]{3,2,1,0:T(2,128)(2,1)}, u32[]{:S(2)}) copy-start(bf16[512,2,1,512]{3,2,1,0:T(2,128)(2,1)} %get-tuple-element.18) | copy-start | bytes 3145732
  239.4 11.3 %copy-start.18 = (s32[128,8]{0,1:T(8,128)S(1)}, s32[128,8]{0,1:T(8,128)}, u32[]{:S(2)}) copy-start(s32[128,8]{0,1:T(8,128)} %param.10) | copy-start | bytes 12292
  248.6 37.7 %collective-permute-start = (bf16[2,512,768]{2,1,0:T(8,128)(2,1)}, bf16[2,512,768]{2,1,0:T(8,128)(2,1)}, u32[]{:S(2)}, u32[]{:S(2)}) collective-permute-start(bf16[2,512,768]{2,1,0:T(8,128)(2,1)} %convolution_convert_fusion.10), channel_id=1, source_target_pairs={{0,8},{8,0},{16,24},{24,16},{1,9},{9,1},{17,25},{25,17},{2,10},{10... | collective-permute-start | bytes 4718600 | tf_op jit(solution)/shard_map/ppermute | solution.py:75
  250.1 69.9 %collective-permute-start.4 = (bf16[2,512,768]{2,1,0:T(8,128)(2,1)}, bf16[2,512,768]{2,1,0:T(8,128)(2,1)}, u32[]{:S(2)}, u32[]{:S(2)}) collective-permute-start(bf16[2,512,768]{2,1,0:T(8,128)(2,1)} %convolution_convert_fusion.6), channel_id=1, source_target_pairs={{0,8},{8,0},{16,24},{24,16},{1,9},{9,1},{17,25},{25,17},{2,10},{10... | collective-permute-start | bytes 4718600 | tf_op jit(solution)/shard_map/ppermute | solution.py:75
  251.3 4.9 %copy-start.8 = (bf16[2,512,768]{2,1,0:T(8,128)(2,1)S(1)}, bf16[2,512,768]{2,1,0:T(8,128)(2,1)}, u32[]{:S(2)}) copy-start(bf16[2,512,768]{2,1,0:T(8,128)(2,1)} %copy-done.7) | copy-start | bytes 4718596
  251.3 102.3 %collective-permute-start.8 = (bf16[2,512,768]{2,1,0:T(8,128)(2,1)}, bf16[2,512,768]{2,1,0:T(8,128)(2,1)S(1)}, u32[]{:S(2)}, u32[]{:S(2)}) collective-permute-start(bf16[2,512,768]{2,1,0:T(8,128)(2,1)} %convolution_convert_fusion.2), channel_id=1, source_target_pairs={{0,8},{8,0},{16,24},{24,16},{1,9},{9,1},{17,25},{25,17},{2,10},{10... | collective-permute-start | bytes 4718600 | tf_op jit(solution)/shard_map/ppermute | solution.py:75
  255.5 27.0 %copy-start.4 = (bf16[2,512,768]{2,1,0:T(8,128)(2,1)S(1)}, bf16[2,512,768]{2,1,0:T(8,128)(2,1)}, u32[]{:S(2)}) copy-start(bf16[2,512,768]{2,1,0:T(8,128)(2,1)} %get-tuple-element.10) | copy-start | bytes 4718596
  255.5 27.0 %copy-start.10 = (bf16[512,1,2,512]{0,3,2,1:T(8,128)(2,1)S(1)}, bf16[512,1,2,512]{0,3,2,1:T(8,128)(2,1)}, u32[]{:S(2)}) copy-start(bf16[512,1,2,512]{0,3,2,1:T(8,128)(2,1)} %copy.94) | copy-start | bytes 3145732
  255.6 114.9 %collective-permute-start.7 = (bf16[512,768]{1,0:T(8,128)(2,1)S(1)}, bf16[512,768]{1,0:T(8,128)(2,1)S(1)}, u32[]{:S(2)}, u32[]{:S(2)}) collective-permute-start(bf16[512,768]{1,0:T(8,128)(2,1)S(1)} %fusion.30), channel_id=1, source_target_pairs={{0,8},{8,0},{16,24},{24,16},{1,9},{9,1},{17,25},{25,17},{2,10},{10... | collective-permute-start | bytes 2359304 | tf_op jit(solution)/shard_map/ppermute | solution.py:75
  281.1 106.2 %collective-permute-start.3 = (bf16[512,768]{1,0:T(8,128)(2,1)S(1)}, bf16[512,768]{1,0:T(8,128)(2,1)S(1)}, u32[]{:S(2)}, u32[]{:S(2)}) collective-permute-start(bf16[512,768]{1,0:T(8,128)(2,1)S(1)} %fusion.28), channel_id=1, source_target_pairs={{0,8},{8,0},{16,24},{24,16},{1,9},{9,1},{17,25},{25,17},{2,10},{10... | collective-permute-start | bytes 2359304 | tf_op jit(solution)/shard_map/ppermute | solution.py:75
  285.1 35.5 %copy-start.6 = (bf16[2,512,768]{2,1,0:T(8,128)(2,1)S(1)}, bf16[2,512,768]{2,1,0:T(8,128)(2,1)}, u32[]{:S(2)}) copy-start(bf16[2,512,768]{2,1,0:T(8,128)(2,1)} %copy-done.5) | copy-start | bytes 4718596
  286.3 116.3 %collective-permute-start.11 = (bf16[512,768]{1,0:T(8,128)(2,1)S(1)}, bf16[512,768]{1,0:T(8,128)(2,1)S(1)}, u32[]{:S(2)}, u32[]{:S(2)}) collective-permute-start(bf16[512,768]{1,0:T(8,128)(2,1)S(1)} %fusion.32), channel_id=1, source_target_pairs={{0,8},{8,0},{16,24},{24,16},{1,9},{9,1},{17,25},{25,17},{2,10},{10... | collective-permute-start | bytes 2359304 | tf_op jit(solution)/shard_map/ppermute | solution.py:75
  320.0 67.5 %collective-permute-start.1 = (bf16[512,768]{1,0:T(8,128)(2,1)S(1)}, bf16[512,768]{1,0:T(8,128)(2,1)S(1)}, u32[]{:S(2)}, u32[]{:S(2)}) collective-permute-start(bf16[512,768]{1,0:T(8,128)(2,1)S(1)} %fusion.27), channel_id=1, source_target_pairs={{0,16},{8,24},{16,0},{24,8},{1,17},{9,25},{17,1},{25,9},{2,18},{10... | collective-permute-start | bytes 2359304 | tf_op jit(solution)/shard_map/ppermute | solution.py:75
  353.6 34.1 %collective-permute-start.5 = (bf16[512,768]{1,0:T(8,128)(2,1)S(1)}, bf16[512,768]{1,0:T(8,128)(2,1)S(1)}, u32[]{:S(2)}, u32[]{:S(2)}) collective-permute-start(bf16[512,768]{1,0:T(8,128)(2,1)S(1)} %fusion.29), channel_id=1, source_target_pairs={{0,16},{8,24},{16,0},{24,8},{1,17},{9,25},{17,1},{25,9},{2,18},{10... | collective-permute-start | bytes 2359304 | tf_op jit(solution)/shard_map/ppermute | solution.py:75
  370.5 32.3 %collective-permute-start.9 = (bf16[512,768]{1,0:T(8,128)(2,1)S(1)}, bf16[512,768]{1,0:T(8,128)(2,1)S(1)}, u32[]{:S(2)}, u32[]{:S(2)}) collective-permute-start(bf16[512,768]{1,0:T(8,128)(2,1)S(1)} %fusion.31), channel_id=1, source_target_pairs={{0,16},{8,24},{16,0},{24,8},{1,17},{9,25},{17,1},{25,9},{2,18},{10... | collective-permute-start | bytes 2359304 | tf_op jit(solution)/shard_map/ppermute | solution.py:75
  (5 other events, 18.2 us)
Sparse Core Ops, SparseCore 0:
  9.6 49.8 all-gather.2
  61.1 46.0 all-gather.4
  197.8 50.3 reduce-scatter.1
